TPU v7x, 32 devices: a whole 2x2x4 slice. The times are simulated.
32 devices in a mesh: groups: 2 (over y), ctx: 4 (over z), head: 2 (over x), sub: 2 (over core).
Axes of the slice: x: 2, y: 2, z: 4, core: 2. Of those that a mesh axis runs over, the one named last changes fastest.
Arguments:
- tokens: bfloat16 [16384, 3584], P(('groups', 'ctx', 'sub'), 'head'), parts along dimension 0, may hold values from -40 to 40
- q_weight: bfloat16 [3584, 3584], P('sub', 'head'), may hold values from -0.09375 to 0.09375
- k_weight: bfloat16 [3584, 512], P('sub', 'head'), may hold values from -0.09375 to 0.09375
- v_weight: bfloat16 [3584, 512], P('sub', 'head'), may hold values from -0.09375 to 0.09375
- q_bias: float32 [3584], P('head'), may hold values from -3 to 3
- v_bias: float32 [512], P('head'), may hold values from -3 to 3
Outputs:
- head_outputs: bfloat16 [16384, 3584], P(('groups', 'ctx', 'sub')), parts along dimension 0
There are 2 independent parts, one for each index of `groups`. A program takes and returns all parts, laid end to end along the dimension named above; an argument that names none is the same for every part. Nothing has to cross between parts.
All inputs are finite; a program needn't handle non-finite values.
Results may differ from a plain program's by a relative error of at most 0.0059.
Values may be sent and summed in bfloat16 or wider, within the bound.
A program may use at most 128 MiB of HBM per device.

v0:
```python
import math

import jax
import jax.numpy as jnp
from jax import lax
from jax.sharding import PartitionSpec as P

HQ = 28
KVH = 4
HD = 128
BLOCK = 128


def from_behind(value, axis, steps):
    count = lax.axis_size(axis)
    first, last = (max(0, -steps), min(count, count - steps))
    return lax.ppermute(value, axis, [(source, source + steps) for source in range(first, last)])


def rotate(values, positions):
    half = values.shape[-1] // 2
    freqs = jnp.exp(-(2.0 * jnp.arange(half, dtype=jnp.float32) / (2 * half)) * math.log(1000000.0))
    angle = positions[:, None] * freqs[None, :]
    cosine = jnp.cos(angle)[:, None, :]
    sine = jnp.sin(angle)[:, None, :]
    first = values[..., :half]
    second = values[..., half:]
    return jnp.concatenate(
        [first * cosine - second * sine, second * cosine + first * sine], axis=-1
    )


def attend(operands):
    query_group, keys, vals, mask = operands
    scores = jnp.einsum(
        "bqkgd,bskd->bkgqs", query_group, keys, preferred_element_type=jnp.float32
    ) * (1.0 / math.sqrt(HD))
    scores = jnp.where(mask[:, None, None], scores, -1e30)
    peak = jnp.max(scores, axis=-1, keepdims=True)
    expo = jnp.exp(scores - peak)
    weights = (expo / jnp.sum(expo, axis=-1, keepdims=True)).astype(jnp.bfloat16)
    return jnp.einsum(
        "bkgqs,bskd->bqkgd", weights, vals, preferred_element_type=jnp.float32
    ).astype(jnp.bfloat16)


def on_device(tokens, q_weight, k_weight, v_weight, q_bias, v_bias):
    q_full, k_full, v_full = (
        lax.all_gather(q_weight, "sub", axis=0, tiled=True),
        lax.all_gather(k_weight, "sub", axis=0, tiled=True),
        lax.all_gather(v_weight, "sub", axis=0, tiled=True),
    )
    rows = tokens.shape[0]
    heads_local = k_full.shape[1] // HD
    group = HQ // KVH
    accumulate_piece = lax.all_gather(tokens, "head", axis=1, tiled=True)
    q_acc = jnp.dot(accumulate_piece, q_full, preferred_element_type=jnp.float32)
    k_acc = jnp.dot(accumulate_piece, k_full, preferred_element_type=jnp.float32)
    v_acc = jnp.dot(accumulate_piece, v_full, preferred_element_type=jnp.float32)
    n_sub = lax.axis_size("sub")
    n_ctx = lax.axis_size("ctx")
    my_shard = lax.axis_index("ctx") * n_sub + lax.axis_index("sub")
    positions = (my_shard * rows + jnp.arange(rows, dtype=jnp.int32)).astype(jnp.float32)
    query = rotate(
        (q_acc + q_bias[None, :]).reshape(rows, heads_local * group, HD), positions
    ).astype(jnp.bfloat16)
    keyed = rotate(k_acc.reshape(rows, heads_local, HD), positions).astype(jnp.bfloat16)
    valued = (v_acc + v_bias[None, :]).astype(jnp.bfloat16).reshape(rows, heads_local, HD)
    paired = jnp.stack([keyed, valued])
    before = from_behind(paired, ("ctx", "sub"), 1)
    reach = [step for step in (1, 2, 4, 8) if step < n_ctx]
    collected = lax.all_gather(paired, "ctx", axis=1, tiled=True)
    ctx_place = lax.axis_index("ctx")
    distant = [
        lax.dynamic_slice_in_dim(collected, jnp.maximum(ctx_place - step, 0) * rows, rows, 1)
        for step in reach
    ]
    distant = distant + [jnp.zeros_like(paired) for missing in range(4 - len(reach))]
    blocks = rows // BLOCK
    nearby = jnp.concatenate([before, paired], axis=1).reshape(
        2, 2 * blocks, BLOCK, heads_local, HD
    )
    near_steps = (0, 1, 2, 4, blocks)
    slots = [nearby[:, blocks - step : 2 * blocks - step] for step in near_steps]
    slots = slots + [piece.reshape(2, blocks, BLOCK, heads_local, HD) for piece in distant]
    selected = jnp.stack(slots, axis=2).reshape(2, blocks, 9 * BLOCK, heads_local, HD)
    far_steps = tuple((n_sub * blocks * step for step in (1, 2, 4, 8)))
    distances = jnp.array(near_steps + far_steps, dtype=jnp.int32)
    global_block = my_shard * blocks + jnp.arange(blocks, dtype=jnp.int32)
    valid = global_block[:, None] - distances[None, :] >= 0
    lower = (
        jnp.arange(BLOCK, dtype=jnp.int32)[:, None] >= jnp.arange(BLOCK, dtype=jnp.int32)[None, :]
    )
    notself = jnp.arange(9, dtype=jnp.int32) != 0
    mask = valid[:, None, :, None] & (notself[None, None, :, None] | lower[None, :, None, :])
    mask = mask.reshape(blocks, BLOCK, 9 * BLOCK)
    halves = 2
    per_half = blocks // halves
    query_blocks = query.reshape(halves, per_half, BLOCK, heads_local, group, HD)
    keys = selected[0].reshape(halves, per_half, 9 * BLOCK, heads_local, HD)
    vals = selected[1].reshape(halves, per_half, 9 * BLOCK, heads_local, HD)
    mask = mask.reshape(halves, per_half, BLOCK, 9 * BLOCK)
    result = lax.map(attend, (query_blocks, keys, vals, mask))
    local_out = result.reshape(rows, heads_local * group * HD)
    return lax.all_gather(local_out, "head", axis=1, tiled=True)


def solution(mesh):
    return jax.shard_map(
        on_device,
        mesh=mesh,
        in_specs=(
            P(("groups", "ctx", "sub"), "head"),
            P("sub", "head"),
            P("sub", "head"),
            P("sub", "head"),
            P("head"),
            P("head"),
        ),
        out_specs=P(("groups", "ctx", "sub"), None),
        check_vma=False,
    )
```

profile of v0, /device:TPU:0, one launch (start us, length us, event | category | flops | bytes accessed | tf_op | source)
XLA Modules:
  0.0 449.1 jit_solution(7114747541433823364)
XLA Ops:
  6.5 0.7 all-gather.9.cloned.1.call-update
  7.3 0.0 all-gather.7.cloned.1.call-start
  7.3 0.7 all-gather.7.cloned.1.call-update
  8.0 0.0 all-gather.11.cloned.1.call-start
  8.1 0.7 all-gather.11.cloned.1.call-update
  8.7 0.0 all-gather.15.cloned.1.call-start
  8.8 0.5 all-gather.15.cloned.1.call-update
  9.3 0.0 all-gather.13.cloned.1.call-start
  9.4 1.0 multiply_cosine_fusion
  10.4 1.0 copy.38
  11.4 1.0 copy.40
  12.4 9.4 %all-gather.9.cloned.1.call-done = bf16[3584,256]{1,0:T(8,128)(2,1)} async-done(((bf16[1792,256]{1,0:T(8,128)(2,1)}), bf16[3584,256]{1,0:T(8,128)(2,1)}) %all-gather.9.cloned.1.call-update) | async-done | bytes 1835024 | tf_op jit(solution)/shard_map/all_gather | solution.py:50
  21.8 94.9 %all-gather.7.cloned.1.call-done = bf16[1024,3584]{1,0:T(8,128)(2,1)} async-done(((bf16[1024,1792]{1,0:T(8,128)(2,1)}), bf16[1024,3584]{1,0:T(8,128)(2,1)}) %all-gather.7.cloned.1.call-update) | async-done | bytes 7340048 | tf_op jit(solution)/shard_map/all_gather | solution.py:56
  116.8 5.7 %fusion.46 = f32[1024,256]{0,1:T(8,128)S(1)} fusion(bf16[1024,3584]{1,0:T(8,128)(2,1)} %all-gather.7.cloned.1.call-done, bf16[3584,256]{1,0:T(8,128)(2,1)} %all-gather.9.cloned.1.call-done), kind=kOutput, calls=%fused_computation.70 | convolution fusion | flops 1879048192 | bytes 10223616 | tf_op jit(solution)/shard_map/dot_general | solution.py:58
  122.5 0.1 fusion.45
  122.5 0.3 copy.61
  122.9 1.3 copy.62
  124.2 4.3 all-gather.11.cloned.1.call-done
  128.5 5.7 %fusion.30 = bf16[1024,256]{0,1:T(8,128)(2,1)S(1)} fusion(bf16[1024,3584]{1,0:T(8,128)(2,1)} %all-gather.7.cloned.1.call-done, bf16[3584,256]{1,0:T(8,128)(2,1)} %all-gather.11.cloned.1.call-done, f32[256]{0:T(256)S(1)} %copy-done.2), kind=kOutput, calls=%fused_computation.35 | convolution fusion | flops 1879572480 | bytes 9700352 | tf_op jit(solution)/shard_map/dot_general | solution.py:59
  134.3 0.3 copy.41
  134.5 1.8 fusion.36
  136.3 1.3 pad_maximum_fusion.1
  137.6 3.1 collective-permute-start
  140.7 0.1 add_compare_fusion
  140.8 0.1 and.20
  141.0 0.1 broadcast_bitcast_fusion
  141.0 0.2 bitcast_or_fusion
  141.3 1.7 broadcast_and_fusion
  143.0 0.0 all-gather.13.cloned.1.call-update
  143.0 0.2 all-gather.17.cloned.1.call-start
  143.3 1.9 maximum_maximum_fusion
  145.1 1.3 fusion.44
  146.4 1.2 fusion.35
  147.6 1.1 fusion.34
  148.7 1.2 fusion.33
  149.9 1.2 fusion.32
  151.1 1.2 fusion.31
  152.2 4.1 all-gather.15.cloned.1.call-done
  156.3 20.7 %convolution_add_fusion = f32[1024,1792]{1,0:T(8,128)} fusion(bf16[1024,3584]{1,0:T(8,128)(2,1)} %all-gather.7.cloned.1.call-done, bf16[3584,1792]{1,0:T(8,128)(2,1)} %all-gather.15.cloned.1.call-done, f32[1792]{0:T(1024)S(1)} %copy-done.1), kind=kOutput, calls=%fused_computation.28 | convolution fusion | flops 13155172352 | bytes 27532288 | tf_op jit(solution)/shard_map/dot_general | solution.py:57
  177.0 8.4 %copy.49 = f32[1024,1792]{0,1:T(8,128)} copy(f32[1024,1792]{1,0:T(8,128)} %convolution_add_fusion) | data formatting | bytes 14680064 | tf_op jit(solution)/shard_map/add | solution.py:65
  185.4 6.3 %subtract_convert_fusion = (bf16[1024,14,64]{0,2,1:T(8,128)(2,1)}, bf16[1024,14,64]{0,2,1:T(8,128)(2,1)}) fusion(f32[1024,14,128]{0,2,1:T(8,128)} %bitcast.103, f32[1024,64]{0,1:T(8,128)S(1)} %get-tuple-element.80, f32[1024,64]{0,1:T(8,128)S(1)} %get-tuple-element.79), kind=kLoop, calls=%fused_computation.31 | loop fusion | flops 7340032 | bytes 11534336 | tf_op jit(solution)/shard_map/convert.7
  191.7 3.6 concatenate.31
  195.2 4.5 concatenate.32
  199.7 5.7 %pad_maximum_fusion = bf16[2,4,128,2,7,128]{2,1,0,5,4,3:T(4,128)(2,1)} fusion(bf16[2,4,128,2,7,64]{2,1,0,5,4,3:T(4,128)(2,1)} %concatenate.32, bf16[2,4,128,2,7,64]{2,1,0,5,4,3:T(4,128)(2,1)S(1)} %concatenate.31), kind=kLoop, calls=%fused_computation.29 | loop fusion | flops 1835008 | bytes 7340032 | tf_op jit(solution)/shard_map/concatenate | solution.py:28
  205.4 34.3 %all-gather.13.cloned.1.call-done = bf16[2,4096,2,128]{3,1,2,0:T(8,128)(2,1)} async-done(((bf16[2,1024,2,128]{3,1,2,0:T(8,128)(2,1)}), bf16[2,4096,2,128]{3,1,2,0:T(8,128)(2,1)}) %all-gather.13.cloned.1.call-update) | async-done | bytes 4194320 | tf_op jit(solution)/shard_map/all_gather | solution.py:72
  239.7 1.8 constant_dynamic-slice_fusion.1
  241.5 1.2 copy_dynamic-update-slice_fusion.2
  242.7 1.1 copy_dynamic-update-slice_fusion.1
  243.8 1.8 broadcast_dynamic-update-slice_fusion
  245.6 11.8 %fusion.43 = (bf16[1,8,9,128,2,128]{5,3,2,4,1,0:T(8,128)(2,1)}, bf16[1,8,9,128,2,128]{5,3,2,4,1,0:T(8,128)(2,1)}) fusion(bf16[2,8,9,128,2,128]{5,3,2,4,1,0:T(8,128)(2,1)} %broadcast_dynamic-update-slice_fusion), kind=kLoop, calls=%fused_computation.67 | loop fusion | bytes 18874368 | tf_op jit(solution)/shard_map/slice | solution.py:100
  257.4 77.0 %while.10 = (s32[]{:T(128)}, bf16[2,4,128,2,7,128]{2,1,0,5,4,3:T(4,128)(2,1)}, bf16[2,4,1152,2,128]{4,2,3,1,0:T(8,128)(2,1)}, pred[2,4,128,1152]{2,3,1,0:T(8,128...) while((s32[]{:T(128)}, ...), condition=%wide.region_3.4_spmd, body=%wide.region_0.3_spmd.sunk | while | flops 4278322176 | bytes 87287376 | solution.py:103
  257.4 2.2 constant_dynamic-slice_fusion.4
  259.7 3.0 copy.89
  262.8 17.6 %fusion.60 = (f32[4,2,7,128]{3,2,1,0:T(8,128)S(1)}, f32[4,2,7,128,1152]{3,4,2,1,0:T(8,128)}) fusion(pred[4,128,1152]{1,2,0:T(8,128)(4,1)S(1)} %dynamic-slice_bitcast_fusion.2, bf16[2,4,1152,2,128]{4,2,3,1,0:T(8,128)(2,1)} %get-tuple-element.140, s32[]{:T(128)} %get-tuple-element.129, bf16[1,4,128,2,7,128]{5,2,4,3,1,0:T(8,128)(2,1)} %copy.89), kind=kOutput, calls=%fused_computation.66.clone.1 | convolution fusion | flops 2146960512 | bytes 37843456 | tf_op jit(solution)/shard_map/while/body/eval_jaxpr/sub | solution.py:40
  280.3 12.9 %convert_bitcast_fusion.2 = bf16[1,4,128,2,7,128]{2,5,4,3,1,0:T(8,128)(2,1)S(1)} fusion(f32[4,2,7,128,1152]{3,4,2,1,0:T(8,128)} %get-tuple-element.120, f32[4,2,7,128]{3,2,1,0:T(8,128)S(1)} %get-tuple-element.121, bf16[2,4,1152,2,128]{4,2,3,1,0:T(8,128)(2,1)} %get-tuple-element.138, s32[]{:T(128)} %get-tuple-element.129), kind=kOutput, calls=%fused_computation.21.clone.1 | convolution fusion | flops 2131361792 | bytes 37253632 | tf_op jit(solution)/shard_map/while/body/eval_jaxpr/bkgqs,bskd->bqkgd/dot_general | solution.py:42
  293.2 2.8 copy_dynamic-update-slice_fusion.4
  296.0 2.2 constant_dynamic-slice_fusion.4
  298.2 3.0 copy.89
  301.3 17.6 %fusion.60 = (f32[4,2,7,128]{3,2,1,0:T(8,128)S(1)}, f32[4,2,7,128,1152]{3,4,2,1,0:T(8,128)}) fusion(pred[4,128,1152]{1,2,0:T(8,128)(4,1)S(1)} %dynamic-slice_bitcast_fusion.2, bf16[2,4,1152,2,128]{4,2,3,1,0:T(8,128)(2,1)} %get-tuple-element.140, s32[]{:T(128)} %get-tuple-element.129, bf16[1,4,128,2,7,128]{5,2,4,3,1,0:T(8,128)(2,1)} %copy.89), kind=kOutput, calls=%fused_computation.66.clone.1 | convolution fusion | flops 2146960512 | bytes 37843456 | tf_op jit(solution)/shard_map/while/body/eval_jaxpr/sub | solution.py:40
  318.8 12.9 %convert_bitcast_fusion.2 = bf16[1,4,128,2,7,128]{2,5,4,3,1,0:T(8,128)(2,1)S(1)} fusion(f32[4,2,7,128,1152]{3,4,2,1,0:T(8,128)} %get-tuple-element.120, f32[4,2,7,128]{3,2,1,0:T(8,128)S(1)} %get-tuple-element.121, bf16[2,4,1152,2,128]{4,2,3,1,0:T(8,128)(2,1)} %get-tuple-element.138, s32[]{:T(128)} %get-tuple-element.129), kind=kOutput, calls=%fused_computation.21.clone.1 | convolution fusion | flops 2131361792 | bytes 37253632 | tf_op jit(solution)/shard_map/while/body/eval_jaxpr/bkgqs,bskd->bqkgd/dot_general | solution.py:42
  331.7 2.7 copy_dynamic-update-slice_fusion.4
  334.4 7.1 %reshape.179 = bf16[1024,1792]{0,1:T(8,128)(2,1)} reshape(bf16[2,4,128,2,7,128]{2,1,0,5,4,3:T(4,128)(2,1)} %get-tuple-element.37) | data formatting | bytes 7340032 | tf_op jit(solution)/shard_map/reshape | solution.py:104
  341.5 90.8 %all-gather.17.cloned.1.call-done = bf16[1024,3584]{0,1:T(8,128)(2,1)} async-done(((bf16[1024,1792]{0,1:T(8,128)(2,1)}), bf16[1024,3584]{0,1:T(8,128)(2,1)}) %all-gather.17.cloned.1.call-update) | async-done | bytes 7340048 | tf_op jit(solution)/shard_map/all_gather | solution.py:105
  432.3 9.9 %copy.53 = bf16[1024,3584]{1,0:T(8,128)(2,1)} copy(bf16[1024,3584]{0,1:T(8,128)(2,1)} %all-gather.17.cloned.1.call-done) | data formatting | bytes 14680064 | tf_op jit(solution)/shard_map/all_gather | solution.py:105
  (18 shorter events, 0.2 us)
Async XLA Ops:
  6.5 15.3 %all-gather.9.cloned.1.call-start = ((), (), s32[]{:S(2)}) async-start(), calls=%async_computation.1 | async-start | bytes 2752512 | tf_op jit(solution)/shard_map/all_gather | solution.py:50
  7.3 109.5 %all-gather.7.cloned.1.call-start = ((), (), s32[]{:S(2)}) async-start(), calls=%async_computation | async-start | bytes 11010048 | tf_op jit(solution)/shard_map/all_gather | solution.py:56
  8.0 120.5 %all-gather.11.cloned.1.call-start = ((), (), s32[]{:S(2)}) async-start(), calls=%async_computation.2 | async-start | bytes 2752512 | tf_op jit(solution)/shard_map/all_gather | solution.py:51
  8.7 147.6 %all-gather.15.cloned.1.call-start = ((), (), s32[]{:S(2)}) async-start(), calls=%async_computation.4 | async-start | bytes 19267584 | tf_op jit(solution)/shard_map/all_gather | solution.py:49
  9.3 230.4 %all-gather.13.cloned.1.call-start = ((), (), s32[]{:S(2)}) async-start(), calls=%async_computation.3 | async-start | bytes 5242880 | tf_op jit(solution)/shard_map/all_gather | solution.py:72
  122.5 6.1 %copy-start.2 = (f32[256]{0:T(256)S(1)}, f32[256]{0:T(256)}, u32[]{:S(2)}) copy-start(f32[256]{0:T(256)} %param.14) | copy-start | bytes 3076
  134.2 6.5 %copy-start = (s32[9]{0:T(128)S(1)}, s32[9]{0:T(128)}, u32[]{:S(2)}) copy-start(s32[9]{0:T(128)} %constant.61) | copy-start | bytes 112
  137.6 5.7 %collective-permute-start = (bf16[2,1024,2,128]{3,1,2,0:T(8,128)(2,1)}, bf16[2,1024,2,128]{3,1,2,0:T(8,128)(2,1)}, u32[]{:S(2)}, u32[]{:S(2)}) collective-permute-start(bf16[2,1024,2,128]{3,1,2,0:T(8,128)(2,1)} %pad_maximum_fusion.1), channel_id=1, source_target_pairs={{0,1},{1,4},{4,5},{5,8},{8,9},{9,12},{12,13},{2,3},{3,6},{6,7},{7,... | collective-permute-start | bytes 3145736 | tf_op jit(solution)/shard_map/ppermute | solution.py:17
  143.0 289.3 %all-gather.17.cloned.1.call-start = ((), (), s32[]{:S(2)}) async-start(), calls=%async_computation.5 | async-start | bytes 11010048 | tf_op jit(solution)/shard_map/all_gather | solution.py:105
  147.6 8.7 %copy-start.1 = (f32[1792]{0:T(1024)S(1)}, f32[1792]{0:T(1024)}, u32[]{:S(2)}) copy-start(f32[1792]{0:T(1024)} %param.13) | copy-start | bytes 21508
Sparse Core Ops, SparseCore 0:
  8.9 12.8 all-gather.8
  23.4 93.3 all-gather.6
  118.3 10.1 all-gather.10
  130.0 26.3 all-gather.14
  157.7 81.9 all-gather.12
  341.7 90.6 all-gather.16
where the time goes:
time: 450 us; the launch traced here: 449 us
  waiting for transfers between devices  241 us (54%)
  matrix products  92.9 us (21%)
  local copies, waits for them, and re-layouts  78.5 us (17%)
  other arithmetic  19.9 us (4%)
  between operations  13.6 us (3%)
    all_gather x1, waiting for transfers between devices, on_device(): accumulate_piece = lax.all_gather(tokens, 'head', axis=1, tiled=True)  94.9 us
    all_gather x1, waiting for transfers between devices, on_device(): return lax.all_gather(local_out, 'head', axis=1, tiled=True)  90.8 us
    sub x2, matrix products, attend(): expo = jnp.exp(scores - peak)  35.1 us
    all_gather x1, waiting for transfers between devices, on_device(): collected = lax.all_gather(paired, 'ctx', axis=1, tiled=True)  34.3 us
    dot_general x2, matrix products, attend(): jnp.einsum('bkgqs,bskd->bqkgd', weights, vals, preferred_element_type=jnp...  25.7 us
    dot_general x1, matrix products, on_device(): jnp.dot(accumulate_piece, q_full, preferred_element_type=jnp.float32)  20.7 us
    slice x1, local copies, waits for them, and re-layouts, on_device(): keys = selected[0].reshape(halves, per_half, 9 * BLOCK, heads_local, HD)  11.8 us
    dynamic_slice x4, local copies, waits for them, and re-layouts, on_device(): result = lax.map(attend, (query_blocks, keys, vals, mask))  10.6 us
  transfers between devices with their start and end apart: 7, of which 6 were waited for; matrix products, arithmetic and copies ran while one was open for 18% of the time, Pallas kernels for 0%

commit v1 on v0

v1 whole, which is shorter than its diff:
```python
import functools
import math

import jax
import jax.numpy as jnp
from jax import lax
from jax.experimental import pallas as pl
from jax.experimental.pallas import tpu as pltpu
from jax.sharding import PartitionSpec as P

HQ = 28
KVH = 4
HD = 128
BLOCK = 128
DISTANCES = (0, 1, 2, 4, 8, 16, 32, 64, 128)
MESH = pl.DeviceIdType.MESH
PAIR = 2


def angle_tables(my_shard, rows):
    half = HD // 2
    freqs = jnp.exp(-(2.0 * jnp.arange(half, dtype=jnp.float32) / (2 * half)) * math.log(1000000.0))
    starts = my_shard * rows + BLOCK * jnp.arange(rows // BLOCK, dtype=jnp.int32)
    points = jnp.concatenate([starts, jnp.arange(BLOCK, dtype=jnp.int32)]).astype(jnp.float32)
    angle = points[:, None] * freqs[None, :]
    cosine, sine = jnp.cos(angle), jnp.sin(angle)
    return jnp.concatenate([cosine, cosine], axis=1), jnp.concatenate([sine, sine], axis=1)


def kernel(
    sizes, tok_ref, wq_ref, wk_ref, wv_ref, qb_ref, vb_ref, cos_ref, sin_ref, out_ref,
    tok, weight, query, kv, staged, kcat, vcat,
    w_load, t_load, w_send, w_recv, t_send, t_recv, kv_send, kv_recv, o_store, o_send, o_recv,
):
    n_ctx, n_head, n_sub = sizes
    n_shards = n_ctx * n_sub
    rows, feats = tok_ref.shape
    w_rows, q_cols = wq_ref.shape
    kv_cols = wk_ref.shape[1]
    hl = kv_cols // HD
    group = HQ // KVH
    nb = rows // BLOCK
    pairs = nb // PAIR
    part = PAIR * BLOCK
    me_x = lax.axis_index("head")
    me_s = lax.axis_index("sub")
    shard = lax.axis_index("ctx") * n_sub + me_s
    near = [d for d in DISTANCES if 0 < d < nb]
    far = [d // nb for d in DISTANCES if d >= nb and d // nb < n_shards]

    def shard_id(step):
        target = lax.rem(shard + step + n_shards, n_shards)
        return {"ctx": target // n_sub, "sub": lax.rem(target, n_sub)}

    def head_id(step):
        return {"head": lax.rem(me_x + step, n_head)}

    def sub_id(step):
        return {"sub": lax.rem(me_s + step, n_sub)}

    barrier = pltpu.get_barrier_semaphore()
    for step in range(1, n_head):
        pl.semaphore_signal(barrier, inc=1, device_id=head_id(step), device_id_type=MESH)
    for step in range(1, n_sub):
        pl.semaphore_signal(barrier, inc=1, device_id=sub_id(step), device_id_type=MESH)
    for step in far:
        pl.semaphore_signal(barrier, inc=1, device_id=shard_id(-step), device_id_type=MESH)

    mine = pl.ds(pl.multiple_of(me_s * w_rows, w_rows), w_rows)
    sources = (
        (wk_ref, pl.ds(q_cols, kv_cols)),
        (wv_ref, pl.ds(q_cols + kv_cols, kv_cols)),
        (wq_ref, pl.ds(0, q_cols)),
    )
    w_loads = [
        pltpu.make_async_copy(ref, weight.at[mine, cols], w_load.at[i])
        for i, (ref, cols) in enumerate(sources)
    ]
    t_own = pltpu.make_async_copy(tok_ref, tok.at[me_x], t_load)
    for copy in w_loads:
        copy.start()
    t_own.start()
    pl.semaphore_wait(barrier, n_head - 1 + n_sub - 1 + len(far))

    def token_copy(step, c):
        piece = pl.ds(pl.multiple_of(c * part, part), part)
        return pltpu.make_async_remote_copy(
            src_ref=tok_ref.at[piece], dst_ref=tok.at[me_x, piece],
            send_sem=t_send.at[step - 1, c], recv_sem=t_recv.at[step - 1, c],
            device_id=head_id(step), device_id_type=MESH,
        )

    def weight_copy(step, i):
        ref, cols = sources[i]
        return pltpu.make_async_remote_copy(
            src_ref=ref, dst_ref=weight.at[mine, cols],
            send_sem=w_send.at[step - 1, i], recv_sem=w_recv.at[step - 1, i],
            device_id=sub_id(step), device_id_type=MESH,
        )

    for c in range(pairs):
        for step in range(1, n_head):
            token_copy(step, c).start()
        if c == 0:
            for i in range(len(sources)):
                for step in range(1, n_sub):
                    weight_copy(step, i).start()

    def kv_copy(i, c):
        return pltpu.make_async_remote_copy(
            src_ref=kv.at[0, pl.ds(c * PAIR, PAIR)],
            dst_ref=kv.at[i + 1, pl.ds(c * PAIR, PAIR)],
            send_sem=kv_send.at[i, c], recv_sem=kv_recv.at[i, c],
            device_id=shard_id(far[i]), device_id_type=MESH,
        )

    vcat[:, HD:] = jnp.ones((vcat.shape[0], HD), vcat.dtype)
    sign = jnp.where(lax.broadcasted_iota(jnp.int32, (1, HD), 1) < HD // 2, -1.0, 1.0)

    def project(c, cols):
        piece = pl.ds(pl.multiple_of(c * part, part), part)
        total = None
        for h in range(n_head):
            term = jnp.dot(
                tok[h, piece, :], weight[h * feats:(h + 1) * feats, cols],
                preferred_element_type=jnp.float32,
            )
            total = term if total is None else total + term
        return total

    def angles(c):
        found = []
        for b in range(PAIR):
            cb, sb = cos_ref[pl.ds(c * PAIR + b, 1), :], sin_ref[pl.ds(c * PAIR + b, 1), :]
            cr, sr = cos_ref[nb:, :], sin_ref[nb:, :]
            found.append((cb * cr - sb * sr, (sb * cr + cb * sr) * sign))
        return found

    def rotated(value, angle):
        return (value * angle[0] + pltpu.roll(value, HD // 2, 1) * angle[1]).astype(jnp.bfloat16)

    tile = 2 * HD if q_cols % (2 * HD) == 0 else HD

    def project_part(c):
        for step in range(1, n_head):
            token_copy(step, c).wait_recv()
        angle = angles(c)
        made = project(c, pl.ds(q_cols, 2 * kv_cols))
        for b in range(PAIR):
            lines = slice(b * BLOCK, (b + 1) * BLOCK)
            for g in range(hl):
                kv[0, c * PAIR + b, g] = rotated(made[lines, g * HD:(g + 1) * HD], angle[b])
                cols = slice(g * HD, (g + 1) * HD)
                moved = made[lines, kv_cols + g * HD:kv_cols + (g + 1) * HD] + vb_ref[:, cols]
                kv[0, c * PAIR + b, hl + g] = moved.astype(jnp.bfloat16)
        for i in range(len(far)):
            kv_copy(i, c).start()

        def columns(t, carry):
            cols = pl.ds(pl.multiple_of(t * tile, tile), tile)
            value = project(c, cols) + qb_ref[:, cols]
            for b in range(PAIR):
                for u in range(tile // HD):
                    query[c * PAIR + b, t * (tile // HD) + u] = rotated(
                        value[b * BLOCK:(b + 1) * BLOCK, u * HD:(u + 1) * HD], angle[b]
                    )
            return carry

        lax.fori_loop(0, q_cols // tile, columns, 0)

    scale = math.log2(math.e) / math.sqrt(HD)
    lower = lax.broadcasted_iota(jnp.int32, (BLOCK, BLOCK), 0) >= lax.broadcasted_iota(
        jnp.int32, (BLOCK, BLOCK), 1
    )

    def out_copies(j):
        lines = pl.ds(pl.multiple_of(j * BLOCK, BLOCK), BLOCK)
        place = out_ref.at[lines, pl.ds(pl.multiple_of(me_x * q_cols, HD), q_cols)]
        local = pltpu.make_async_copy(staged.at[lines], place, o_store.at[j])
        sends = [
            pltpu.make_async_remote_copy(
                src_ref=staged.at[lines], dst_ref=place,
                send_sem=o_send.at[step - 1, j], recv_sem=o_recv.at[step - 1, j],
                device_id=head_id(step), device_id_type=MESH,
            )
            for step in range(1, n_head)
        ]
        return local, sends

    def attend_block(j):
        slots = [(0, j, None)]
        for d in near:
            inside = j >= d
            slots.append((jnp.where(inside, 0, 1), lax.rem(j - d + nb, nb), inside | (shard >= 1)))
        for i, step in enumerate(far):
            slots.append((i + 1, j, shard >= step))
        bias = [None if ok is None else jnp.where(ok, 0.0, -1e30) for _, _, ok in slots]
        lines = pl.ds(pl.multiple_of(j * BLOCK, BLOCK), BLOCK)

        def one_group(g, carry):
            for s, (source, block, _) in enumerate(slots):
                kcat[s * BLOCK:(s + 1) * BLOCK, :] = kv[source, block, g]
                vcat[s * BLOCK:(s + 1) * BLOCK, :HD] = kv[source, block, hl + g]
            for h in range(group):
                scores = lax.dot_general(
                    query[j, g * group + h], kcat[...], (((1,), (1,)), ((), ())),
                    preferred_element_type=jnp.float32,
                )
                pieces = []
                for s in range(len(slots)):
                    piece = scores[:, s * BLOCK:(s + 1) * BLOCK] * scale
                    pieces.append(
                        jnp.where(lower, piece, -1e30) if s == 0 else piece + bias[s]
                    )
                peak = jnp.max(functools.reduce(jnp.maximum, pieces), axis=1, keepdims=True)
                expo = jnp.concatenate(
                    [jnp.exp2(piece - peak).astype(jnp.bfloat16) for piece in pieces], axis=1
                )
                summed = jnp.dot(expo, vcat[...], preferred_element_type=jnp.float32)
                cols = pl.ds(pl.multiple_of((g * group + h) * HD, HD), HD)
                staged[lines, cols] = (summed[:, :HD] / summed[:, HD:]).astype(jnp.bfloat16)
            return carry

        lax.fori_loop(0, hl, one_group, 0)
        local, sends = out_copies(j)
        for copy in sends:
            copy.start()
        local.start()

    def attend_pair(c):
        for i in range(len(far)):
            kv_copy(i, c).wait_recv()

        def one_block(b, carry):
            attend_block(c * PAIR + b)
            return carry

        lax.fori_loop(0, PAIR, one_block, 0)

    t_own.wait()
    for copy in w_loads:
        copy.wait()
    for i in range(len(sources)):
        for step in range(1, n_sub):
            weight_copy(step, i).wait_recv()

    first = max(near) // PAIR

    def turn(i, carry):
        @pl.when(i < pairs)
        def _():
            project_part(i)

        @pl.when(i >= first)
        def _():
            attend_pair(lax.rem(i, pairs))

        return carry

    lax.fori_loop(0, pairs + first, turn, 0)

    for i in range(len(sources)):
        for step in range(1, n_sub):
            weight_copy(step, i).wait_send()
    for c in range(pairs):
        for step in range(1, n_head):
            token_copy(step, c).wait_send()
        for i in range(len(far)):
            kv_copy(i, c).wait_send()
    for j in range(nb):
        local, sends = out_copies(j)
        local.wait()
        for copy in sends:
            copy.wait()


def on_device(sizes, tokens, q_weight, k_weight, v_weight, q_bias, v_bias):
    n_ctx, n_head, n_sub = sizes
    n_shards = n_ctx * n_sub
    rows, feats = tokens.shape
    w_rows, q_cols = q_weight.shape
    kv_cols = k_weight.shape[1]
    hl = kv_cols // HD
    nb = rows // BLOCK
    pairs = nb // PAIR
    n_far = len([d for d in DISTANCES if d >= nb and d // nb < n_shards])
    n_slots = len([d for d in DISTANCES if d < nb]) + n_far
    cosine, sine = angle_tables(lax.axis_index("ctx") * n_sub + lax.axis_index("sub"), rows)
    full = w_rows * n_sub
    total = q_cols + 2 * kv_cols
    dma = pltpu.SemaphoreType.DMA
    anywhere = pl.BlockSpec(memory_space=pl.ANY)
    inside = pl.BlockSpec(memory_space=pltpu.VMEM)
    return pl.pallas_call(
        functools.partial(kernel, sizes),
        out_shape=jax.ShapeDtypeStruct((rows, q_cols * n_head), jnp.bfloat16),
        in_specs=[anywhere] * 4 + [inside] * 4,
        out_specs=anywhere,
        scratch_shapes=[
            pltpu.VMEM((n_head, rows, feats), jnp.bfloat16),
            pltpu.VMEM((full, total), jnp.bfloat16),
            pltpu.VMEM((nb, q_cols // HD, BLOCK, HD), jnp.bfloat16),
            pltpu.VMEM((n_far + 1, nb, 2 * hl, BLOCK, HD), jnp.bfloat16),
            pltpu.VMEM((rows, q_cols), jnp.bfloat16),
            pltpu.VMEM((n_slots * BLOCK, HD), jnp.bfloat16),
            pltpu.VMEM((n_slots * BLOCK, 2 * HD), jnp.bfloat16),
            dma((3,)), dma,
            dma((n_sub - 1, 3)), dma((n_sub - 1, 3)),
            dma((n_head - 1, pairs)), dma((n_head - 1, pairs)),
            dma((n_far, pairs)), dma((n_far, pairs)),
            dma((nb,)), dma((n_head - 1, nb)), dma((n_head - 1, nb)),
        ],
        compiler_params=pltpu.CompilerParams(
            collective_id=0, has_side_effects=True, vmem_limit_bytes=60 * 1024 * 1024
        ),
    )(
        tokens, q_weight, k_weight, v_weight,
        q_bias.reshape(1, -1), v_bias.reshape(1, -1), cosine, sine,
    )


def solution(mesh):
    sizes = (mesh.shape["ctx"], mesh.shape["head"], mesh.shape["sub"])
    return jax.shard_map(
        functools.partial(on_device, sizes),
        mesh=mesh,
        in_specs=(
            P(("groups", "ctx", "sub"), "head"),
            P("sub", "head"),
            P("sub", "head"),
            P("sub", "head"),
            P("head"),
            P("head"),
        ),
        out_specs=P(("groups", "ctx", "sub"), None),
        check_vma=False,
    )
```

time: 450 us -> 182 us (0.40)
  waiting for transfers between devices: 241 us -> 0 us
  Pallas kernels: 0 us -> 173 us
  matrix products: 92.9 us -> 0 us
  local copies, waits for them, and re-layouts: 78.5 us -> 7.9 us
  other arithmetic: 19.9 us -> 1.17 us
  between operations: 13.6 us -> 0.02 us
    all_gather x6 -> x0, waiting for transfers between devices: 238 us -> none  [the longest x1 94.9 us: on_device(): accumulate_piece = lax.all_gather(tokens, 'head', axis=1, tiled=True)]
    pallas_call x0 -> x1, Pallas kernels: none -> 173 us  [on_device(): pl.pallas_call(functools.partial(kernel, sizes), out_shape=jax.ShapeDtype...]
    dot_general x5 -> x0, matrix products: 57.8 us -> none  [the longest x2 25.7 us: attend(): jnp.einsum('bkgqs,bskd->bqkgd', weights, vals, preferred_element_type=jnp...]
    sub x2 -> x0, matrix products: 35.1 us -> none  [attend(): expo = jnp.exp(scores - peak)]
    slice x3 -> x0, local copies, waits for them, and re-layouts: 13.2 us -> none  [the longest x1 11.8 us: on_device(): keys = selected[0].reshape(halves, per_half, 9 * BLOCK, heads_local, HD)]
    dynamic_slice x5 -> x0, local copies, waits for them, and re-layouts: 12.3 us -> none  [the longest x4 10.6 us: on_device(): result = lax.map(attend, (query_blocks, keys, vals, mask))]
    all_gather x1 -> x0, local copies, waits for them, and re-layouts: 9.93 us -> none  [on_device(): return lax.all_gather(local_out, 'head', axis=1, tiled=True)]
    concatenate x3 -> x1, other arithmetic: 9.33 us -> 0.76 us  [angle_tables(): jnp.concatenate([cosine, cosine], axis=1)]
  transfers between devices with their start and end apart: 7 -> 0, of which waited for: 6 -> 0; matrix products, arithmetic and copies ran while one was open for 18% -> 0% of each run, Pallas kernels for 0% -> 0%
where the time goes in v1:
time: 182 us
  Pallas kernels  173 us (95%)
  local copies, waits for them, and re-layouts  7.9 us (4%)
    pallas_call x1, Pallas kernels, on_device(): pl.pallas_call(functools.partial(kernel, sizes), out_shape=jax.ShapeDtype...  173 us
    unnamed x1, local copies, waits for them, and re-layouts  6.6 us

profile of v1, /device:TPU:0, one launch (start us, length us, event | category | flops | bytes accessed | tf_op | source)
XLA Modules:
  0.0 181.8 jit_solution(68127202314197925)
XLA Ops:
  0.0 0.1 add_convert_fusion
  0.1 1.3 reshape.24.qb_ref
  1.4 0.3 multiply_sine_fusion
  1.7 0.8 pad_maximum_fusion
  2.5 172.7 %shard_map.64 = bf16[1024,3584]{1,0:T(8,128)(2,1)} custom-call(bf16[1024,1792]{1,0:T(8,128)(2,1)} %tok_ref.1, bf16[1792,1792]{1,0:T(8,128)(2,1)} %wq_ref.1, bf16[1792,256]{1,0:T(8,128)(2,1)} %wk_ref.1, bf16[1792,256]{1,0:T(8,128)(2,1)} %wv_ref.1, f32[1,1792]{1,0:T(1,128)} %reshape.24.qb_ref, f32[1,256]{1,0:T(1,128)} %bitcast.1, ...), custom_call_target="tpu_custom_call" | custom-call | tf_op jit(solution)/shard_map/pallas_call | solution.py:294
  175.2 6.6 %copy.8 = bf16[1024,3584]{1,0:T(8,128)(2,1)} copy(bf16[1024,3584]{1,0:T(8,128)(2,1)} %shard_map.64) | data formatting | bytes 14680064
  (3 shorter events, 0.0 us)

commit v2 on v1

--- a/solution.py
+++ b/solution.py
@@ -14,21 +14,24 @@
 BLOCK = 128
 DISTANCES = (0, 1, 2, 4, 8, 16, 32, 64, 128)
 MESH = pl.DeviceIdType.MESH
-PAIR = 2
-
-
-def angle_tables(my_shard, rows):
+PAIR = 1
+
+
+def small_table(my_shard, rows, q_bias, v_bias):
     half = HD // 2
     freqs = jnp.exp(-(2.0 * jnp.arange(half, dtype=jnp.float32) / (2 * half)) * math.log(1000000.0))
+    freqs = jnp.concatenate([freqs, freqs])
     starts = my_shard * rows + BLOCK * jnp.arange(rows // BLOCK, dtype=jnp.int32)
-    points = jnp.concatenate([starts, jnp.arange(BLOCK, dtype=jnp.int32)]).astype(jnp.float32)
-    angle = points[:, None] * freqs[None, :]
-    cosine, sine = jnp.cos(angle), jnp.sin(angle)
-    return jnp.concatenate([cosine, cosine], axis=1), jnp.concatenate([sine, sine], axis=1)
+    inner = jnp.arange(BLOCK, dtype=jnp.int32).astype(jnp.float32)[:, None] * freqs[None, :]
+    outer = starts.astype(jnp.float32)[:, None] * freqs[None, :]
+    return jnp.concatenate([
+        jnp.cos(inner), jnp.sin(inner), jnp.cos(outer), jnp.sin(outer),
+        q_bias.reshape(-1, HD), v_bias.reshape(-1, HD),
+    ])
 
 
 def kernel(
-    sizes, tok_ref, wq_ref, wk_ref, wv_ref, qb_ref, vb_ref, cos_ref, sin_ref, out_ref,
+    sizes, tok_ref, wq_ref, wk_ref, wv_ref, table, out_ref,
     tok, weight, query, kv, staged, kcat, vcat,
     w_load, t_load, w_send, w_recv, t_send, t_recv, kv_send, kv_recv, o_store, o_send, o_recv,
 ):
@@ -42,6 +45,8 @@
     nb = rows // BLOCK
     pairs = nb // PAIR
     part = PAIR * BLOCK
+    heads = q_cols // HD
+    bias_at = 2 * (BLOCK + nb)
     me_x = lax.axis_index("head")
     me_s = lax.axis_index("sub")
     shard = lax.axis_index("ctx") * n_sub + me_s
@@ -131,8 +136,9 @@
     def angles(c):
         found = []
         for b in range(PAIR):
-            cb, sb = cos_ref[pl.ds(c * PAIR + b, 1), :], sin_ref[pl.ds(c * PAIR + b, 1), :]
-            cr, sr = cos_ref[nb:, :], sin_ref[nb:, :]
+            block = c * PAIR + b
+            cb, sb = table[pl.ds(2 * BLOCK + block, 1), :], table[pl.ds(2 * BLOCK + nb + block, 1), :]
+            cr, sr = table[:BLOCK, :], table[BLOCK:2 * BLOCK, :]
             found.append((cb * cr - sb * sr, (sb * cr + cb * sr) * sign))
         return found
 
@@ -150,21 +156,26 @@
             lines = slice(b * BLOCK, (b + 1) * BLOCK)
             for g in range(hl):
                 kv[0, c * PAIR + b, g] = rotated(made[lines, g * HD:(g + 1) * HD], angle[b])
-                cols = slice(g * HD, (g + 1) * HD)
-                moved = made[lines, kv_cols + g * HD:kv_cols + (g + 1) * HD] + vb_ref[:, cols]
+                moved = made[lines, kv_cols + g * HD:kv_cols + (g + 1) * HD] + table[pl.ds(bias_at + heads + g, 1), :]
                 kv[0, c * PAIR + b, hl + g] = moved.astype(jnp.bfloat16)
         for i in range(len(far)):
             kv_copy(i, c).start()
 
         def columns(t, carry):
             cols = pl.ds(pl.multiple_of(t * tile, tile), tile)
-            value = project(c, cols) + qb_ref[:, cols]
+            value = project(c, cols)
             for b in range(PAIR):
                 for u in range(tile // HD):
-                    query[c * PAIR + b, t * (tile // HD) + u] = rotated(
-                        value[b * BLOCK:(b + 1) * BLOCK, u * HD:(u + 1) * HD], angle[b]
+                    head = t * (tile // HD) + u
+                    part_value = value[b * BLOCK:(b + 1) * BLOCK, u * HD:(u + 1) * HD]
+                    query[c * PAIR + b, head] = rotated(
+                        part_value + table[pl.ds(bias_at + head, 1), :], angle[b]
                     )
             return carry
+
+        @pl.when(c == 0)
+        def _():
+            wait_weights((2,))
 
         lax.fori_loop(0, q_cols // tile, columns, 0)
 
@@ -237,12 +248,14 @@
 
         lax.fori_loop(0, PAIR, one_block, 0)
 
+    def wait_weights(chosen):
+        for i in chosen:
+            w_loads[i].wait()
+            for step in range(1, n_sub):
+                weight_copy(step, i).wait_recv()
+
     t_own.wait()
-    for copy in w_loads:
-        copy.wait()
-    for i in range(len(sources)):
-        for step in range(1, n_sub):
-            weight_copy(step, i).wait_recv()
+    wait_weights((0, 1))
 
     first = max(near) // PAIR
 
@@ -251,13 +264,13 @@
         def _():
             project_part(i)
 
-        @pl.when(i >= first)
+        @pl.when(i > first)
         def _():
-            attend_pair(lax.rem(i, pairs))
+            attend_pair(lax.rem(i - 1, pairs))
 
         return carry
 
-    lax.fori_loop(0, pairs + first, turn, 0)
+    lax.fori_loop(0, pairs + first + 1, turn, 0)
 
     for i in range(len(sources)):
         for step in range(1, n_sub):
@@ -285,7 +298,7 @@
     pairs = nb // PAIR
     n_far = len([d for d in DISTANCES if d >= nb and d // nb < n_shards])
     n_slots = len([d for d in DISTANCES if d < nb]) + n_far
-    cosine, sine = angle_tables(lax.axis_index("ctx") * n_sub + lax.axis_index("sub"), rows)
+    my_shard = lax.axis_index("ctx") * n_sub + lax.axis_index("sub")
     full = w_rows * n_sub
     total = q_cols + 2 * kv_cols
     dma = pltpu.SemaphoreType.DMA
@@ -294,7 +307,7 @@
     return pl.pallas_call(
         functools.partial(kernel, sizes),
         out_shape=jax.ShapeDtypeStruct((rows, q_cols * n_head), jnp.bfloat16),
-        in_specs=[anywhere] * 4 + [inside] * 4,
+        in_specs=[anywhere] * 4 + [inside],
         out_specs=anywhere,
         scratch_shapes=[
             pltpu.VMEM((n_head, rows, feats), jnp.bfloat16),
@@ -314,8 +327,7 @@
             collective_id=0, has_side_effects=True, vmem_limit_bytes=60 * 1024 * 1024
         ),
     )(
-        tokens, q_weight, k_weight, v_weight,
-        q_bias.reshape(1, -1), v_bias.reshape(1, -1), cosine, sine,
+        tokens, q_weight, k_weight, v_weight, small_table(my_shard, rows, q_bias, v_bias),
     )
 
 

time: 182 us -> 178 us (0.978)
  Pallas kernels: 173 us -> 165 us
  local copies, waits for them, and re-layouts: 7.9 us -> 11.6 us
    pallas_call x1, Pallas kernels: 173 us -> 165 us  [on_device(): pl.pallas_call(functools.partial(kernel, sizes), out_shape=jax.ShapeDtype...]
    concatenate x0 -> x1, local copies, waits for them, and re-layouts: none -> 5.04 us  [small_table(): jnp.concatenate([jnp.cos(inner), jnp.sin(inner), jnp.cos(outer), jnp.sin(...]
where the time goes in v2:
time: 178 us
  Pallas kernels  165 us (93%)
  local copies, waits for them, and re-layouts  11.6 us (7%)
    pallas_call x1, Pallas kernels, on_device(): pl.pallas_call(functools.partial(kernel, sizes), out_shape=jax.ShapeDtype...  165 us
    unnamed x1, local copies, waits for them, and re-layouts  6.6 us
    concatenate x1, local copies, waits for them, and re-layouts, small_table(): jnp.concatenate([jnp.cos(inner), jnp.sin(inner), jnp.cos(outer), jnp.sin(...  5.04 us

profile of v2, /device:TPU:0, one launch (start us, length us, event | category | flops | bytes accessed | tf_op | source)
XLA Modules:
  0.0 177.5 jit_solution(15289859491459082200)
XLA Ops:
  0.0 0.1 pad_maximum_fusion
  0.1 0.1 multiply_sine_fusion.1
  0.2 0.3 multiply_sine_fusion
  0.5 5.0 %concatenate.7.table = f32[288,128]{1,0:T(8,128)} concatenate(f32[128,128]{1,0:T(8,128)S(1)} %get-tuple-element.8, f32[128,128]{1,0:T(8,128)S(1)} %get-tuple-element.7, f32[8,128]{1,0:T(8,128)S(1)} %get-tuple-element.6, f32[8,128]{1,0:T(8,128)S(1)} %get-tuple-element.5, f32[14,128]{1,0:T(8,128)} %bitcast.2, f32[2,128]{1,0:T(2,128)} %bitcast.3), dimensions={0} | concatenate | bytes 294912 | tf_op jit(solution)/shard_map/concatenate | solution.py:27
  5.6 165.4 %shard_map.64 = bf16[1024,3584]{1,0:T(8,128)(2,1)} custom-call(bf16[1024,1792]{1,0:T(8,128)(2,1)} %tok_ref.1, bf16[1792,1792]{1,0:T(8,128)(2,1)} %wq_ref.1, bf16[1792,256]{1,0:T(8,128)(2,1)} %wk_ref.1, bf16[1792,256]{1,0:T(8,128)(2,1)} %wv_ref.1, f32[288,128]{1,0:T(8,128)} %concatenate.7.table), custom_call_target="tpu_custom_call" | custom-call | tf_op jit(solution)/shard_map/pallas_call | solution.py:307
  170.9 6.6 %copy.8 = bf16[1024,3584]{1,0:T(8,128)(2,1)} copy(bf16[1024,3584]{1,0:T(8,128)(2,1)} %shard_map.64) | data formatting | bytes 14680064
  (3 shorter events, 0.0 us)

commit v3 on v2

--- a/solution.py
+++ b/solution.py
@@ -17,23 +17,20 @@
 PAIR = 1
 
 
-def small_table(my_shard, rows, q_bias, v_bias):
+def angle_tables(my_shard, rows):
     half = HD // 2
-    freqs = jnp.exp(-(2.0 * jnp.arange(half, dtype=jnp.float32) / (2 * half)) * math.log(1000000.0))
-    freqs = jnp.concatenate([freqs, freqs])
+    place = (jnp.arange(HD, dtype=jnp.int32) % half).astype(jnp.float32)
+    freqs = jnp.exp(-(2.0 * place / (2 * half)) * math.log(1000000.0))
     starts = my_shard * rows + BLOCK * jnp.arange(rows // BLOCK, dtype=jnp.int32)
     inner = jnp.arange(BLOCK, dtype=jnp.int32).astype(jnp.float32)[:, None] * freqs[None, :]
     outer = starts.astype(jnp.float32)[:, None] * freqs[None, :]
-    return jnp.concatenate([
-        jnp.cos(inner), jnp.sin(inner), jnp.cos(outer), jnp.sin(outer),
-        q_bias.reshape(-1, HD), v_bias.reshape(-1, HD),
-    ])
+    return jnp.cos(inner), jnp.sin(inner), jnp.cos(outer), jnp.sin(outer)
 
 
 def kernel(
-    sizes, tok_ref, wq_ref, wk_ref, wv_ref, table, out_ref,
-    tok, weight, query, kv, staged, kcat, vcat,
-    w_load, t_load, w_send, w_recv, t_send, t_recv, kv_send, kv_recv, o_store, o_send, o_recv,
+    sizes, tok_ref, wq_ref, wk_ref, wv_ref, cos_in, sin_in, cos_at, sin_at, qb_ref, vb_ref, out_ref,
+    tok, weight, query, kv, kcat, vcat,
+    w_load, t_load, w_send, w_recv, t_send, t_recv, kv_send, kv_recv, o_send, o_recv,
 ):
     n_ctx, n_head, n_sub = sizes
     n_shards = n_ctx * n_sub
@@ -45,8 +42,6 @@
     nb = rows // BLOCK
     pairs = nb // PAIR
     part = PAIR * BLOCK
-    heads = q_cols // HD
-    bias_at = 2 * (BLOCK + nb)
     me_x = lax.axis_index("head")
     me_s = lax.axis_index("sub")
     shard = lax.axis_index("ctx") * n_sub + me_s
@@ -137,8 +132,8 @@
         found = []
         for b in range(PAIR):
             block = c * PAIR + b
-            cb, sb = table[pl.ds(2 * BLOCK + block, 1), :], table[pl.ds(2 * BLOCK + nb + block, 1), :]
-            cr, sr = table[:BLOCK, :], table[BLOCK:2 * BLOCK, :]
+            cb, sb = cos_at[pl.ds(block, 1), :], sin_at[pl.ds(block, 1), :]
+            cr, sr = cos_in[...], sin_in[...]
             found.append((cb * cr - sb * sr, (sb * cr + cb * sr) * sign))
         return found
 
@@ -156,7 +151,7 @@
             lines = slice(b * BLOCK, (b + 1) * BLOCK)
             for g in range(hl):
                 kv[0, c * PAIR + b, g] = rotated(made[lines, g * HD:(g + 1) * HD], angle[b])
-                moved = made[lines, kv_cols + g * HD:kv_cols + (g + 1) * HD] + table[pl.ds(bias_at + heads + g, 1), :]
+                moved = made[lines, kv_cols + g * HD:kv_cols + (g + 1) * HD] + vb_ref[pl.ds(g, 1), :]
                 kv[0, c * PAIR + b, hl + g] = moved.astype(jnp.bfloat16)
         for i in range(len(far)):
             kv_copy(i, c).start()
@@ -169,7 +164,7 @@
                     head = t * (tile // HD) + u
                     part_value = value[b * BLOCK:(b + 1) * BLOCK, u * HD:(u + 1) * HD]
                     query[c * PAIR + b, head] = rotated(
-                        part_value + table[pl.ds(bias_at + head, 1), :], angle[b]
+                        part_value + qb_ref[pl.ds(head, 1), :], angle[b]
                     )
             return carry
 
@@ -187,16 +182,14 @@
     def out_copies(j):
         lines = pl.ds(pl.multiple_of(j * BLOCK, BLOCK), BLOCK)
         place = out_ref.at[lines, pl.ds(pl.multiple_of(me_x * q_cols, HD), q_cols)]
-        local = pltpu.make_async_copy(staged.at[lines], place, o_store.at[j])
-        sends = [
+        return [
             pltpu.make_async_remote_copy(
-                src_ref=staged.at[lines], dst_ref=place,
+                src_ref=place, dst_ref=place,
                 send_sem=o_send.at[step - 1, j], recv_sem=o_recv.at[step - 1, j],
                 device_id=head_id(step), device_id_type=MESH,
             )
             for step in range(1, n_head)
         ]
-        return local, sends
 
     def attend_block(j):
         slots = [(0, j, None)]
@@ -228,15 +221,13 @@
                     [jnp.exp2(piece - peak).astype(jnp.bfloat16) for piece in pieces], axis=1
                 )
                 summed = jnp.dot(expo, vcat[...], preferred_element_type=jnp.float32)
-                cols = pl.ds(pl.multiple_of((g * group + h) * HD, HD), HD)
-                staged[lines, cols] = (summed[:, :HD] / summed[:, HD:]).astype(jnp.bfloat16)
+                cols = pl.ds(pl.multiple_of(me_x * q_cols + (g * group + h) * HD, HD), HD)
+                out_ref[lines, cols] = (summed[:, :HD] / summed[:, HD:]).astype(jnp.bfloat16)
             return carry
 
         lax.fori_loop(0, hl, one_group, 0)
-        local, sends = out_copies(j)
-        for copy in sends:
+        for copy in out_copies(j):
             copy.start()
-        local.start()
 
     def attend_pair(c):
         for i in range(len(far)):
@@ -281,9 +272,7 @@
         for i in range(len(far)):
             kv_copy(i, c).wait_send()
     for j in range(nb):
-        local, sends = out_copies(j)
-        local.wait()
-        for copy in sends:
+        for copy in out_copies(j):
             copy.wait()
 
 
@@ -302,32 +291,32 @@
     full = w_rows * n_sub
     total = q_cols + 2 * kv_cols
     dma = pltpu.SemaphoreType.DMA
-    anywhere = pl.BlockSpec(memory_space=pl.ANY)
+    far_memory = pl.BlockSpec(memory_space=pltpu.HBM)
     inside = pl.BlockSpec(memory_space=pltpu.VMEM)
     return pl.pallas_call(
         functools.partial(kernel, sizes),
-        out_shape=jax.ShapeDtypeStruct((rows, q_cols * n_head), jnp.bfloat16),
-        in_specs=[anywhere] * 4 + [inside],
-        out_specs=anywhere,
+        out_shape=pltpu.VMEM((rows, q_cols * n_head), jnp.bfloat16),
+        in_specs=[far_memory] * 4 + [inside] * 6,
+        out_specs=inside,
         scratch_shapes=[
             pltpu.VMEM((n_head, rows, feats), jnp.bfloat16),
             pltpu.VMEM((full, total), jnp.bfloat16),
             pltpu.VMEM((nb, q_cols // HD, BLOCK, HD), jnp.bfloat16),
             pltpu.VMEM((n_far + 1, nb, 2 * hl, BLOCK, HD), jnp.bfloat16),
-            pltpu.VMEM((rows, q_cols), jnp.bfloat16),
             pltpu.VMEM((n_slots * BLOCK, HD), jnp.bfloat16),
             pltpu.VMEM((n_slots * BLOCK, 2 * HD), jnp.bfloat16),
             dma((3,)), dma,
             dma((n_sub - 1, 3)), dma((n_sub - 1, 3)),
             dma((n_head - 1, pairs)), dma((n_head - 1, pairs)),
             dma((n_far, pairs)), dma((n_far, pairs)),
-            dma((nb,)), dma((n_head - 1, nb)), dma((n_head - 1, nb)),
+            dma((n_head - 1, nb)), dma((n_head - 1, nb)),
         ],
         compiler_params=pltpu.CompilerParams(
-            collective_id=0, has_side_effects=True, vmem_limit_bytes=60 * 1024 * 1024
+            collective_id=0, has_side_effects=True, vmem_limit_bytes=54 * 1024 * 1024
         ),
     )(
-        tokens, q_weight, k_weight, v_weight, small_table(my_shard, rows, q_bias, v_bias),
+        tokens, q_weight, k_weight, v_weight, *angle_tables(my_shard, rows),
+        q_bias.reshape(-1, HD), v_bias.reshape(-1, HD),
     )
 
 

time: 178 us -> 170 us (0.955)
  local copies, waits for them, and re-layouts: 11.6 us -> 3.05 us
    concatenate x1 -> x0, local copies, waits for them, and re-layouts: 5.04 us -> none  [small_table(): jnp.concatenate([jnp.cos(inner), jnp.sin(inner), jnp.cos(outer), jnp.sin(...]
    unnamed x1, local copies, waits for them, and re-layouts: 6.6 us -> 3.05 us
where the time goes in v3:
time: 170 us
  Pallas kernels  165 us (97%)
  local copies, waits for them, and re-layouts  3.05 us (2%)
    pallas_call x1, Pallas kernels, on_device(): pl.pallas_call(functools.partial(kernel, sizes), out_shape=pltpu.VMEM((ro...  165 us

profile of v3, /device:TPU:0, one launch (start us, length us, event | category | flops | bytes accessed | tf_op | source)
XLA Modules:
  0.0 169.9 jit_solution(13036085489630357957)
XLA Ops:
  0.0 0.7 multiply_sine_fusion.1
  0.7 0.9 multiply_sine_fusion
  1.7 165.1 %shard_map.64 = bf16[1024,3584]{1,0:T(8,128)(2,1)S(1)} custom-call(bf16[1024,1792]{1,0:T(8,128)(2,1)} %tok_ref.1, bf16[1792,1792]{1,0:T(8,128)(2,1)} %wq_ref.1, bf16[1792,256]{1,0:T(8,128)(2,1)} %wk_ref.1, bf16[1792,256]{1,0:T(8,128)(2,1)} %wv_ref.1, f32[128,128]{1,0:T(8,128)} %get-tuple-element.8.cos_in, f32[128,128]{1,0:T(8,128)} %get-tuple-element.7.sin_in, ...), custom_call_target="tpu_custom_call" | custom-call | tf_op jit(solution)/shard_map/pallas_call | solution.py:296
  166.8 3.1 %copy.8 = bf16[1024,3584]{1,0:T(8,128)(2,1)} copy(bf16[1024,3584]{1,0:T(8,128)(2,1)S(1)} %shard_map.64) | data formatting | bytes 14680064
  (3 shorter events, 0.0 us)

commit v4 on v3

--- a/solution.py
+++ b/solution.py
@@ -98,10 +98,25 @@
             device_id=sub_id(step), device_id_type=MESH,
         )
 
-    for c in range(pairs):
+    mid = max(near)
+    order, attended = [], {}
+    for j in range(mid, nb):
+        order += [b for b in sorted(j - d for d in [0] + near) if b not in order]
+        attended[len(order)] = j
+    for j in range(mid):
+        attended[max(attended) + 1] = j
+    turns = max(attended) + 1
+
+    def chosen_by(i, table, otherwise):
+        found = otherwise
+        for at, value in table:
+            found = jnp.where(i == at, value, found)
+        return found
+
+    for c in order:
         for step in range(1, n_head):
             token_copy(step, c).start()
-        if c == 0:
+        if c == order[0]:
             for i in range(len(sources)):
                 for step in range(1, n_sub):
                     weight_copy(step, i).start()
@@ -168,7 +183,7 @@
                     )
             return carry
 
-        @pl.when(c == 0)
+        @pl.when(c == order[0])
         def _():
             wait_weights((2,))
 
@@ -179,13 +194,14 @@
         jnp.int32, (BLOCK, BLOCK), 1
     )
 
-    def out_copies(j):
+    def out_copies(j, g):
         lines = pl.ds(pl.multiple_of(j * BLOCK, BLOCK), BLOCK)
-        place = out_ref.at[lines, pl.ds(pl.multiple_of(me_x * q_cols, HD), q_cols)]
+        first_col = pl.multiple_of(me_x * q_cols + g * (group * HD), HD)
+        place = out_ref.at[lines, pl.ds(first_col, group * HD)]
         return [
             pltpu.make_async_remote_copy(
                 src_ref=place, dst_ref=place,
-                send_sem=o_send.at[step - 1, j], recv_sem=o_recv.at[step - 1, j],
+                send_sem=o_send.at[step - 1, j, g], recv_sem=o_recv.at[step - 1, j, g],
                 device_id=head_id(step), device_id_type=MESH,
             )
             for step in range(1, n_head)
@@ -223,21 +239,17 @@
                 summed = jnp.dot(expo, vcat[...], preferred_element_type=jnp.float32)
                 cols = pl.ds(pl.multiple_of(me_x * q_cols + (g * group + h) * HD, HD), HD)
                 out_ref[lines, cols] = (summed[:, :HD] / summed[:, HD:]).astype(jnp.bfloat16)
+            for copy in out_copies(j, g):
+                copy.start()
             return carry
 
         lax.fori_loop(0, hl, one_group, 0)
-        for copy in out_copies(j):
-            copy.start()
-
-    def attend_pair(c):
+
+    def attend_ready(c):
         for i in range(len(far)):
             kv_copy(i, c).wait_recv()
 
-        def one_block(b, carry):
-            attend_block(c * PAIR + b)
-            return carry
-
-        lax.fori_loop(0, PAIR, one_block, 0)
+        attend_block(c)
 
     def wait_weights(chosen):
         for i in chosen:
@@ -248,20 +260,20 @@
     t_own.wait()
     wait_weights((0, 1))
 
-    first = max(near) // PAIR
-
     def turn(i, carry):
         @pl.when(i < pairs)
         def _():
-            project_part(i)
-
-        @pl.when(i > first)
+            project_part(chosen_by(i, list(enumerate(order)), 0))
+
+        block = chosen_by(i, list(attended.items()), -1)
+
+        @pl.when(block >= 0)
         def _():
-            attend_pair(lax.rem(i - 1, pairs))
+            attend_ready(block)
 
         return carry
 
-    lax.fori_loop(0, pairs + first + 1, turn, 0)
+    lax.fori_loop(0, turns, turn, 0)
 
     for i in range(len(sources)):
         for step in range(1, n_sub):
@@ -272,8 +284,9 @@
         for i in range(len(far)):
             kv_copy(i, c).wait_send()
     for j in range(nb):
-        for copy in out_copies(j):
-            copy.wait()
+        for g in range(hl):
+            for copy in out_copies(j, g):
+                copy.wait()
 
 
 def on_device(sizes, tokens, q_weight, k_weight, v_weight, q_bias, v_bias):
@@ -309,7 +322,7 @@
             dma((n_sub - 1, 3)), dma((n_sub - 1, 3)),
             dma((n_head - 1, pairs)), dma((n_head - 1, pairs)),
             dma((n_far, pairs)), dma((n_far, pairs)),
-            dma((n_head - 1, nb)), dma((n_head - 1, nb)),
+            dma((n_head - 1, nb, hl)), dma((n_head - 1, nb, hl)),
         ],
         compiler_params=pltpu.CompilerParams(
             collective_id=0, has_side_effects=True, vmem_limit_bytes=54 * 1024 * 1024

time: 170 us -> 170 us (level)
  no operation moved by 1% of the time
where the time goes in v4:
time: 170 us
  Pallas kernels  165 us (97%)
  local copies, waits for them, and re-layouts  3.05 us (2%)
    pallas_call x1, Pallas kernels, on_device(): pl.pallas_call(functools.partial(kernel, sizes), out_shape=pltpu.VMEM((ro...  165 us

profile of v4, /device:TPU:0, one launch (start us, length us, event | category | flops | bytes accessed | tf_op | source)
XLA Modules:
  0.0 170.0 jit_solution(17419592198751549965)
XLA Ops:
  0.0 0.7 multiply_sine_fusion.1
  0.7 0.9 multiply_sine_fusion
  1.7 165.3 %shard_map.64 = bf16[1024,3584]{1,0:T(8,128)(2,1)S(1)} custom-call(bf16[1024,1792]{1,0:T(8,128)(2,1)} %tok_ref.1, bf16[1792,1792]{1,0:T(8,128)(2,1)} %wq_ref.1, bf16[1792,256]{1,0:T(8,128)(2,1)} %wk_ref.1, bf16[1792,256]{1,0:T(8,128)(2,1)} %wv_ref.1, f32[128,128]{1,0:T(8,128)} %get-tuple-element.8.cos_in, f32[128,128]{1,0:T(8,128)} %get-tuple-element.7.sin_in, ...), custom_call_target="tpu_custom_call" | custom-call | tf_op jit(solution)/shard_map/pallas_call | solution.py:309
  167.0 3.1 %copy.8 = bf16[1024,3584]{1,0:T(8,128)(2,1)} copy(bf16[1024,3584]{1,0:T(8,128)(2,1)S(1)} %shard_map.64) | data formatting | bytes 14680064
  (3 shorter events, 0.0 us)

commit v5 on v4

--- a/solution.py
+++ b/solution.py
@@ -17,20 +17,10 @@
 PAIR = 1
 
 
-def angle_tables(my_shard, rows):
-    half = HD // 2
-    place = (jnp.arange(HD, dtype=jnp.int32) % half).astype(jnp.float32)
-    freqs = jnp.exp(-(2.0 * place / (2 * half)) * math.log(1000000.0))
-    starts = my_shard * rows + BLOCK * jnp.arange(rows // BLOCK, dtype=jnp.int32)
-    inner = jnp.arange(BLOCK, dtype=jnp.int32).astype(jnp.float32)[:, None] * freqs[None, :]
-    outer = starts.astype(jnp.float32)[:, None] * freqs[None, :]
-    return jnp.cos(inner), jnp.sin(inner), jnp.cos(outer), jnp.sin(outer)
-
-
 def kernel(
-    sizes, tok_ref, wq_ref, wk_ref, wv_ref, cos_in, sin_in, cos_at, sin_at, qb_ref, vb_ref, out_ref,
-    tok, weight, query, kv, kcat, vcat,
-    w_load, t_load, w_send, w_recv, t_send, t_recv, kv_send, kv_recv, o_send, o_recv,
+    sizes, tok_ref, wq_ref, wk_ref, wv_ref, qb_hbm, vb_hbm, out_ref,
+    qb_ref, vb_ref, cos_in, sin_in, cos_at, sin_at, tok, weight, query, kv, kcat, vcat,
+    b_load, w_load, t_load, w_send, w_recv, t_send, t_recv, kv_send, kv_recv, o_send, o_recv,
 ):
     n_ctx, n_head, n_sub = sizes
     n_shards = n_ctx * n_sub
@@ -77,9 +67,10 @@
         for i, (ref, cols) in enumerate(sources)
     ]
     t_own = pltpu.make_async_copy(tok_ref, tok.at[me_x], t_load)
-    for copy in w_loads:
-        copy.start()
-    t_own.start()
+    biases = [
+        pltpu.make_async_copy(qb_hbm, qb_ref, b_load.at[0]),
+        pltpu.make_async_copy(vb_hbm, vb_ref, b_load.at[1]),
+    ]
     pl.semaphore_wait(barrier, n_head - 1 + n_sub - 1 + len(far))
 
     def token_copy(step, c):
@@ -121,6 +112,9 @@
                 for step in range(1, n_sub):
                     weight_copy(step, i).start()
 
+    for copy in w_loads + [t_own] + biases:
+        copy.start()
+
     def kv_copy(i, c):
         return pltpu.make_async_remote_copy(
             src_ref=kv.at[0, pl.ds(c * PAIR, PAIR)],
@@ -130,6 +124,13 @@
         )
 
     vcat[:, HD:] = jnp.ones((vcat.shape[0], HD), vcat.dtype)
+    lane = lax.broadcasted_iota(jnp.int32, (1, HD), 1) % (HD // 2)
+    freqs = jnp.exp(-(2.0 * lane.astype(jnp.float32) / HD) * math.log(1000000.0))
+    inner = lax.broadcasted_iota(jnp.int32, (BLOCK, HD), 0).astype(jnp.float32) * freqs
+    cos_in[...], sin_in[...] = jnp.cos(inner), jnp.sin(inner)
+    starts = shard * rows + BLOCK * lax.broadcasted_iota(jnp.int32, (nb, HD), 0)
+    outer = starts.astype(jnp.float32) * freqs
+    cos_at[...], sin_at[...] = jnp.cos(outer), jnp.sin(outer)
     sign = jnp.where(lax.broadcasted_iota(jnp.int32, (1, HD), 1) < HD // 2, -1.0, 1.0)
 
     def project(c, cols):
@@ -257,6 +258,8 @@
             for step in range(1, n_sub):
                 weight_copy(step, i).wait_recv()
 
+    for copy in biases:
+        copy.wait()
     t_own.wait()
     wait_weights((0, 1))
 
@@ -300,7 +303,6 @@
     pairs = nb // PAIR
     n_far = len([d for d in DISTANCES if d >= nb and d // nb < n_shards])
     n_slots = len([d for d in DISTANCES if d < nb]) + n_far
-    my_shard = lax.axis_index("ctx") * n_sub + lax.axis_index("sub")
     full = w_rows * n_sub
     total = q_cols + 2 * kv_cols
     dma = pltpu.SemaphoreType.DMA
@@ -309,16 +311,22 @@
     return pl.pallas_call(
         functools.partial(kernel, sizes),
         out_shape=pltpu.VMEM((rows, q_cols * n_head), jnp.bfloat16),
-        in_specs=[far_memory] * 4 + [inside] * 6,
+        in_specs=[far_memory] * 6,
         out_specs=inside,
         scratch_shapes=[
+            pltpu.VMEM((q_cols // HD, HD), jnp.float32),
+            pltpu.VMEM((hl, HD), jnp.float32),
+            pltpu.VMEM((BLOCK, HD), jnp.float32),
+            pltpu.VMEM((BLOCK, HD), jnp.float32),
+            pltpu.VMEM((nb, HD), jnp.float32),
+            pltpu.VMEM((nb, HD), jnp.float32),
             pltpu.VMEM((n_head, rows, feats), jnp.bfloat16),
             pltpu.VMEM((full, total), jnp.bfloat16),
             pltpu.VMEM((nb, q_cols // HD, BLOCK, HD), jnp.bfloat16),
             pltpu.VMEM((n_far + 1, nb, 2 * hl, BLOCK, HD), jnp.bfloat16),
             pltpu.VMEM((n_slots * BLOCK, HD), jnp.bfloat16),
             pltpu.VMEM((n_slots * BLOCK, 2 * HD), jnp.bfloat16),
-            dma((3,)), dma,
+            dma((2,)), dma((3,)), dma,
             dma((n_sub - 1, 3)), dma((n_sub - 1, 3)),
             dma((n_head - 1, pairs)), dma((n_head - 1, pairs)),
             dma((n_far, pairs)), dma((n_far, pairs)),
@@ -328,7 +336,7 @@
             collective_id=0, has_side_effects=True, vmem_limit_bytes=54 * 1024 * 1024
         ),
     )(
-        tokens, q_weight, k_weight, v_weight, *angle_tables(my_shard, rows),
+        tokens, q_weight, k_weight, v_weight,
         q_bias.reshape(-1, HD), v_bias.reshape(-1, HD),
     )
 

time: 170 us -> 168 us (0.988)
  no operation moved by 1% of the time
where the time goes in v5:
time: 168 us; the launch traced here: 167 us
  Pallas kernels  164 us (98%)
  local copies, waits for them, and re-layouts  3.05 us (2%)
    pallas_call x1, Pallas kernels, on_device(): pl.pallas_call(functools.partial(kernel, sizes), out_shape=pltpu.VMEM((ro...  164 us

profile of v5, /device:TPU:0, one launch (start us, length us, event | category | flops | bytes accessed | tf_op | source)
XLA Modules:
  0.0 167.5 jit_solution(16297014373492191475)
XLA Ops:
  0.0 164.4 %shard_map.64 = bf16[1024,3584]{1,0:T(8,128)(2,1)S(1)} custom-call(bf16[1024,1792]{1,0:T(8,128)(2,1)} %tok_ref.1, bf16[1792,1792]{1,0:T(8,128)(2,1)} %wq_ref.1, bf16[1792,256]{1,0:T(8,128)(2,1)} %wk_ref.1, bf16[1792,256]{1,0:T(8,128)(2,1)} %wv_ref.1, f32[14,128]{1,0:T(8,128)} %bitcast.2, f32[2,128]{1,0:T(2,128)} %bitcast.3), custom_call_target="tpu_custom_call" | custom-call | tf_op jit(solution)/shard_map/pallas_call | solution.py:311
  164.4 3.1 %copy.8 = bf16[1024,3584]{1,0:T(8,128)(2,1)} copy(bf16[1024,3584]{1,0:T(8,128)(2,1)S(1)} %shard_map.64) | data formatting | bytes 14680064

commit v6 on v5

--- a/solution.py
+++ b/solution.py
@@ -123,6 +123,15 @@
             device_id=shard_id(far[i]), device_id_type=MESH,
         )
 
+    for i, step in enumerate(far):
+        @pl.when(shard < step)
+        def _():
+            def clear(block, carry):
+                kv[i + 1, block] = jnp.zeros(kv.shape[2:], kv.dtype)
+                return carry
+
+            lax.fori_loop(0, nb, clear, 0)
+
     vcat[:, HD:] = jnp.ones((vcat.shape[0], HD), vcat.dtype)
     lane = lax.broadcasted_iota(jnp.int32, (1, HD), 1) % (HD // 2)
     freqs = jnp.exp(-(2.0 * lane.astype(jnp.float32) / HD) * math.log(1000000.0))
@@ -169,8 +178,10 @@
                 kv[0, c * PAIR + b, g] = rotated(made[lines, g * HD:(g + 1) * HD], angle[b])
                 moved = made[lines, kv_cols + g * HD:kv_cols + (g + 1) * HD] + vb_ref[pl.ds(g, 1), :]
                 kv[0, c * PAIR + b, hl + g] = moved.astype(jnp.bfloat16)
-        for i in range(len(far)):
-            kv_copy(i, c).start()
+        for i, step in enumerate(far):
+            @pl.when(shard + step < n_shards)
+            def _():
+                kv_copy(i, c).start()
 
         def columns(t, carry):
             cols = pl.ds(pl.multiple_of(t * tile, tile), tile)
@@ -247,8 +258,10 @@
         lax.fori_loop(0, hl, one_group, 0)
 
     def attend_ready(c):
-        for i in range(len(far)):
-            kv_copy(i, c).wait_recv()
+        for i, step in enumerate(far):
+            @pl.when(shard >= step)
+            def _():
+                kv_copy(i, c).wait_recv()
 
         attend_block(c)
 
@@ -284,8 +297,10 @@
     for c in range(pairs):
         for step in range(1, n_head):
             token_copy(step, c).wait_send()
-        for i in range(len(far)):
-            kv_copy(i, c).wait_send()
+        for i, step in enumerate(far):
+            @pl.when(shard + step < n_shards)
+            def _():
+                kv_copy(i, c).wait_send()
     for j in range(nb):
         for g in range(hl):
             for copy in out_copies(j, g):

time: 168 us -> 168 us (level)
  no operation moved by 1% of the time
where the time goes in v6:
time: 168 us; the launch traced here: 167 us
  Pallas kernels  164 us (98%)
  local copies, waits for them, and re-layouts  3.05 us (2%)
    pallas_call x1, Pallas kernels, on_device(): pl.pallas_call(functools.partial(kernel, sizes), out_shape=pltpu.VMEM((ro...  164 us

profile of v6, /device:TPU:0, one launch (start us, length us, event | category | flops | bytes accessed | tf_op | source)
XLA Modules:
  0.0 167.5 jit_solution(14091124191676703337)
XLA Ops:
  0.0 164.4 %shard_map.64 = bf16[1024,3584]{1,0:T(8,128)(2,1)S(1)} custom-call(bf16[1024,1792]{1,0:T(8,128)(2,1)} %tok_ref.1, bf16[1792,1792]{1,0:T(8,128)(2,1)} %wq_ref.1, bf16[1792,256]{1,0:T(8,128)(2,1)} %wk_ref.1, bf16[1792,256]{1,0:T(8,128)(2,1)} %wv_ref.1, f32[14,128]{1,0:T(8,128)} %bitcast.2, f32[2,128]{1,0:T(2,128)} %bitcast.3), custom_call_target="tpu_custom_call" | custom-call | tf_op jit(solution)/shard_map/pallas_call | solution.py:326
  164.4 3.1 %copy.8 = bf16[1024,3584]{1,0:T(8,128)(2,1)} copy(bf16[1024,3584]{1,0:T(8,128)(2,1)S(1)} %shard_map.64) | data formatting | bytes 14680064

commit v7 on v5

--- a/solution.py
+++ b/solution.py
@@ -76,7 +76,7 @@
     def token_copy(step, c):
         piece = pl.ds(pl.multiple_of(c * part, part), part)
         return pltpu.make_async_remote_copy(
-            src_ref=tok_ref.at[piece], dst_ref=tok.at[me_x, piece],
+            src_ref=(tok_ref if c is order[0] else tok.at[me_x]).at[piece], dst_ref=tok.at[me_x, piece],
             send_sem=t_send.at[step - 1, c], recv_sem=t_recv.at[step - 1, c],
             device_id=head_id(step), device_id_type=MESH,
         )
@@ -104,7 +104,10 @@
             found = jnp.where(i == at, value, found)
         return found
 
+    t_own.start()
     for c in order:
+        if len(order) > 1 and c == order[1]:
+            t_own.wait()
         for step in range(1, n_head):
             token_copy(step, c).start()
         if c == order[0]:
@@ -112,7 +115,7 @@
                 for step in range(1, n_sub):
                     weight_copy(step, i).start()
 
-    for copy in w_loads + [t_own] + biases:
+    for copy in w_loads + biases:
         copy.start()
 
     def kv_copy(i, c):
@@ -260,7 +263,6 @@
 
     for copy in biases:
         copy.wait()
-    t_own.wait()
     wait_weights((0, 1))
 
     def turn(i, carry):

time: 168 us -> 168 us (level)
  no operation moved by 1% of the time
where the time goes in v7:
time: 168 us
  Pallas kernels  164 us (98%)
  local copies, waits for them, and re-layouts  3.05 us (2%)
    pallas_call x1, Pallas kernels, on_device(): pl.pallas_call(functools.partial(kernel, sizes), out_shape=pltpu.VMEM((ro...  164 us

profile of v7, /device:TPU:0, one launch (start us, length us, event | category | flops | bytes accessed | tf_op | source)
XLA Modules:
  0.0 167.5 jit_solution(15347395680547091693)
XLA Ops:
  0.0 164.5 %shard_map.64 = bf16[1024,3584]{1,0:T(8,128)(2,1)S(1)} custom-call(bf16[1024,1792]{1,0:T(8,128)(2,1)} %tok_ref.1, bf16[1792,1792]{1,0:T(8,128)(2,1)} %wq_ref.1, bf16[1792,256]{1,0:T(8,128)(2,1)} %wk_ref.1, bf16[1792,256]{1,0:T(8,128)(2,1)} %wv_ref.1, f32[14,128]{1,0:T(8,128)} %bitcast.2, f32[2,128]{1,0:T(2,128)} %bitcast.3), custom_call_target="tpu_custom_call" | custom-call | tf_op jit(solution)/shard_map/pallas_call | solution.py:313
  164.5 3.1 %copy.8 = bf16[1024,3584]{1,0:T(8,128)(2,1)} copy(bf16[1024,3584]{1,0:T(8,128)(2,1)S(1)} %shard_map.64) | data formatting | bytes 14680064
